TPU v7x, 128 devices: a whole 4x4x4 slice. The times are simulated.
128 devices in a mesh: row: 4 (over x), col: 32 (over z, y, core).
Axes of the slice: x: 4, y: 4, z: 4, core: 2. Of those that a mesh axis runs over, the one named last changes fastest.
Arguments:
- tokens: bfloat16 [512, 8192], P('col', 'row'), may hold values from -6 to 6
- out_grad: bfloat16 [512, 8192], P('col', 'row'), may hold values from -6 to 6
- gate_weight: bfloat16 [8192, 29568], P('row', 'col'), may hold values from -0.0625 to 0.0625
- up_weight: bfloat16 [8192, 29568], P('row', 'col'), may hold values from -0.0625 to 0.0625
- down_weight: bfloat16 [29568, 8192], P('col', 'row'), may hold values from -0.03125 to 0.03125
Outputs:
- input_grad: bfloat16 [512, 8192], P('col', 'row')
- gate_wgrad: bfloat16 [8192, 29568], P('row', 'col')
- up_wgrad: bfloat16 [8192, 29568], P('row', 'col')
- down_wgrad: bfloat16 [29568, 8192], P('col', 'row')
All inputs are finite; a program needn't handle non-finite values.
Results may differ from a plain program's by a relative error of at most 0.005.
Values may be sent and summed in bfloat16 or wider, within the bound.
No kernel may reach another device: no remote copies, remote signals or barrier semaphores. Data moves between devices by JAX's collectives and lax.ppermute only.
A program may use at most 128 MiB of HBM per device.

v0:
```python
import math
import jax
import jax.numpy as jnp
from jax import lax
from jax.sharding import PartitionSpec as P


def contract(left, right, left_dim, right_dim):
    return lax.dot_general(
        left, right, (((left_dim,), (right_dim,)), ((), ())), preferred_element_type=jnp.float32
    )


def swiglu_backward(gate, upward, hid_grad):
    sig = jax.nn.sigmoid(gate)
    act = gate * sig
    hidden = (act * upward).astype(jnp.bfloat16)
    gate_grad = (hid_grad * upward * sig * (1.0 + gate * (1.0 - sig))).astype(jnp.bfloat16)
    up_grad = (hid_grad * act).astype(jnp.bfloat16)
    return (hidden, gate_grad, up_grad)


def local(tokens, out_grad, gate_weight, up_weight, down_weight):
    panel_tokens, panel_grads = (
        lax.all_gather(tokens, "col", axis=0, tiled=True),
        lax.all_gather(out_grad, "col", axis=0, tiled=True),
    )
    factor = 1.0 / math.sqrt(panel_tokens.shape[0])
    gate_part = jnp.dot(panel_tokens, gate_weight, preferred_element_type=jnp.float32)
    up_part = jnp.dot(panel_tokens, up_weight, preferred_element_type=jnp.float32)
    grad_part = contract(panel_grads, down_weight, 1, 1)
    gate, upward, hid_grad = lax.psum((gate_part, up_part, grad_part), "row")
    hidden, gate_grad, up_grad = swiglu_backward(gate, upward, hid_grad)
    input_grad = lax.psum_scatter(
        contract(gate_grad, gate_weight, 1, 1) + contract(up_grad, up_weight, 1, 1),
        "col",
        scatter_dimension=0,
        tiled=True,
    ).astype(jnp.bfloat16)
    gate_wgrad = (contract(panel_tokens, gate_grad, 0, 0) * factor).astype(jnp.bfloat16)
    up_wgrad = (contract(panel_tokens, up_grad, 0, 0) * factor).astype(jnp.bfloat16)
    down_wgrad = (contract(hidden, panel_grads, 0, 0) * factor).astype(jnp.bfloat16)
    return (input_grad, gate_wgrad, up_wgrad, down_wgrad)


def solution(mesh):
    placed = (P("col", "row"), P("col", "row"), P("row", "col"), P("row", "col"), P("col", "row"))
    return jax.shard_map(
        local,
        mesh=mesh,
        in_specs=placed,
        out_specs=(P("col", "row"), P("row", "col"), P("row", "col"), P("col", "row")),
        check_vma=False,
    )
```

profile of v0, /device:TPU:0, one launch (start us, length us, event | category | flops | bytes accessed | tf_op | source)
XLA Modules:
  0.0 326.6 jit_solution(14472059379591102396)
XLA Ops:
  7.2 0.0 all-gather.5.cloned.1.call-start
  7.2 0.7 all-gather.5.cloned.1.call-update
  7.9 0.0 all-gather.3.cloned.1.call-start
  7.9 0.7 all-gather.3.cloned.1.call-update
  8.6 0.0 all-reduce.3.cloned.1.call-start
  8.7 48.1 %all-gather.5.cloned.1.call-done = bf16[512,2048]{1,0:T(8,128)(2,1)} async-done(((bf16[16,2048]{1,0:T(8,128)(2,1)}), bf16[512,2048]{1,0:T(8,128)(2,1)}) %all-gather.5.cloned.1.call-update) | async-done | bytes 2097168 | tf_op jit(solution)/shard_map/all_gather | solution.py:25
  56.8 0.0 copy-start
  56.8 0.0 copy-start.5
  56.8 6.3 %fusion.6 = f32[512,924]{0,1:T(8,128)} fusion(bf16[512,2048]{1,0:T(8,128)(2,1)} %all-gather.5.cloned.1.call-done, bf16[2048,924]{0,1:T(8,128)(2,1)} %param.8), kind=kOutput, calls=%fused_computation.13 | convolution fusion | flops 1937768448 | bytes 7774208 | tf_op jit(solution)/shard_map/dot_general | solution.py:30
  63.0 0.0 copy-done
  63.0 0.0 copy-done.5
  63.0 3.4 %fusion.7 = f32[512,924]{0,1:T(8,128)} fusion(bf16[512,2048]{1,0:T(8,128)(2,1)S(1)} %copy-done.5, bf16[2048,924]{0,1:T(8,128)(2,1)S(1)} %copy-done), kind=kOutput, calls=%fused_computation.14 | convolution fusion | flops 1937768448 | bytes 7774208 | tf_op jit(solution)/shard_map/dot_general | solution.py:29
  66.4 35.8 %all-gather.3.cloned.1.call-done = bf16[512,2048]{1,0:T(8,128)(2,1)} async-done(((bf16[16,2048]{1,0:T(8,128)(2,1)}), bf16[512,2048]{1,0:T(8,128)(2,1)}) %all-gather.3.cloned.1.call-update) | async-done | bytes 2097168 | tf_op jit(solution)/shard_map/all_gather | solution.py:26
  102.3 6.1 %fusion.5 = f32[512,924]{0,1:T(8,128)} fusion(bf16[512,2048]{1,0:T(8,128)(2,1)} %all-gather.3.cloned.1.call-done, bf16[924,2048]{1,0:T(8,128)(2,1)} %param.9), kind=kOutput, calls=%fused_computation.12 | convolution fusion | flops 1937768448 | bytes 7774208 | tf_op jit(solution)/shard_map/dot_general | solution.py:9
  108.4 0.0 all-reduce.3.cloned.1.call-update
  108.4 0.2 reduce-scatter.2.cloned.1.call-start
  108.7 116.8 %all-reduce.3.cloned.1.call-done = (f32[512,924]{0,1:T(8,128)}, f32[512,924]{0,1:T(8,128)}, f32[512,924]{0,1:T(8,128)}) async-done(((f32[512,924]{0,1:T(8,128)}, f32[512,924]{0,1:T(8,128)}, f32[512,924]{0,1:T(8,128)}), (f32[512,924]{0,1:T(8,128)}, f32[512,924]{0,1:T(8,128)}, f32[512,924]{0,1:T(8,128)})) %all-reduce.3.cloned.1.call-update) | async-done | bytes 5677072 | tf_op jit(solution)/shard_map/psum | solution.py:32
  225.4 0.0 copy-start.1
  225.4 3.9 %multiply_convert_fusion.4 = (bf16[512,924]{0,1:T(8,128)(2,1)S(1)}, bf16[512,924]{0,1:T(8,128)(2,1)S(1)}) fusion(f32[512,924]{0,1:T(8,128)} %get-tuple-element.5, f32[512,924]{0,1:T(8,128)} %get-tuple-element.4, f32[512,924]{0,1:T(8,128)} %get-tuple-element.6), kind=kLoop, calls=%fused_computation.7 | loop fusion | flops 6150144 | bytes 7569408 | tf_op jit(solution)/shard_map/convert_element_type | solution.py:19
  229.3 0.0 copy-done.1
  229.3 0.0 copy-start.2
  229.3 2.4 fusion.8
  231.8 0.0 copy-done.2
  231.8 4.5 %convolution_add_fusion = f32[512,2048]{1,0:T(8,128)} fusion(f32[512,2048]{1,0:T(8,128)S(1)} %fusion.8, bf16[512,924]{0,1:T(8,128)(2,1)S(1)} %get-tuple-element.7, bf16[2048,924]{0,1:T(8,128)(2,1)S(1)} %copy-done.2), kind=kOutput, calls=%fused_computation.5 | convolution fusion | flops 1938817024 | bytes 13119488 | tf_op jit(solution)/shard_map/dot_general | solution.py:9
  236.3 0.0 reduce-scatter.2.cloned.1.call-update
  236.3 0.0 copy-start.6
  236.3 5.8 %fusion = bf16[2048,924]{0,1:T(8,128)(2,1)} fusion(bf16[512,924]{0,1:T(8,128)(2,1)S(1)} %get-tuple-element.8, bf16[512,2048]{1,0:T(8,128)(2,1)} %all-gather.5.cloned.1.call-done), kind=kOutput, calls=%fused_computation.3 | convolution fusion | flops 1941553152 | bytes 6828032 | tf_op jit(solution)/shard_map/dot_general | solution.py:9
  242.1 0.0 copy-done.6
  242.1 0.0 copy-start.3
  242.1 0.0 copy-start.4
  242.1 0.0 copy-start.7
  242.1 4.1 %fusion.1 = bf16[2048,924]{0,1:T(8,128)(2,1)} fusion(bf16[512,924]{0,1:T(8,128)(2,1)S(1)} %get-tuple-element.7, bf16[512,2048]{1,0:T(8,128)(2,1)S(1)} %copy-done.6), kind=kOutput, calls=%fused_computation.4 | convolution fusion | flops 1941553152 | bytes 6828032 | tf_op jit(solution)/shard_map/dot_general | solution.py:9
  246.2 0.0 copy-done.3
  246.2 0.0 copy-done.4
  246.2 0.0 copy-done.7
  246.2 4.1 %multiply_convert_fusion = bf16[924,2048]{1,0:T(8,128)(2,1)} fusion(bf16[512,2048]{1,0:T(8,128)(2,1)S(1)} %copy-done.7, f32[512,924]{0,1:T(8,128)S(1)} %copy-done.4, f32[512,924]{0,1:T(8,128)S(1)} %copy-done.3), kind=kOutput, calls=%fused_computation | convolution fusion | flops 1944391680 | bytes 9666560 | tf_op jit(solution)/shard_map/dot_general | solution.py:9
  250.3 68.2 %reduce-scatter.2.cloned.1.call-done = f32[16,2048]{1,0:T(8,128)} async-done(((f32[512,2048]{1,0:T(8,128)}), f32[16,2048]{1,0:T(8,128)}) %reduce-scatter.2.cloned.1.call-update) | async-done | bytes 131088 | tf_op jit(solution)/shard_map/reduce_scatter | solution.py:34
  318.5 1.5 convert_element_type.29
Async XLA Ops:
  7.2 49.6 %all-gather.5.cloned.1.call-start = ((), (), s32[]{:S(2)}) async-start(), calls=%async_computation.2 | async-start | bytes 2162688 | tf_op jit(solution)/shard_map/all_gather | solution.py:25
  7.9 94.4 %all-gather.3.cloned.1.call-start = ((), (), s32[]{:S(2)}) async-start(), calls=%async_computation.1 | async-start | bytes 2162688 | tf_op jit(solution)/shard_map/all_gather | solution.py:26
  8.6 216.8 %all-reduce.3.cloned.1.call-start = ((), (), s32[]{:S(2)}) async-start(), calls=%async_computation.4 | async-start | bytes 11403264 | tf_op jit(solution)/shard_map/psum | solution.py:32
  56.8 6.3 %copy-start = (bf16[2048,924]{0,1:T(8,128)(2,1)S(1)}, bf16[2048,924]{0,1:T(8,128)(2,1)}, u32[]{:S(2)}) copy-start(bf16[2048,924]{0,1:T(8,128)(2,1)} %param.7) | copy-start | bytes 11354116
  56.8 6.3 %copy-start.5 = (bf16[512,2048]{1,0:T(8,128)(2,1)S(1)}, bf16[512,2048]{1,0:T(8,128)(2,1)}, u32[]{:S(2)}) copy-start(bf16[512,2048]{1,0:T(8,128)(2,1)} %all-gather.5.cloned.1.call-done) | copy-start | bytes 6291460
  108.4 210.1 %reduce-scatter.2.cloned.1.call-start = ((), (), s32[]{:S(2)}) async-start(), calls=%async_computation.3 | async-start | bytes 4325376 | tf_op jit(solution)/shard_map/reduce_scatter | solution.py:34
  225.4 3.9 %copy-start.1 = (bf16[2048,924]{0,1:T(8,128)(2,1)S(1)}, bf16[2048,924]{0,1:T(8,128)(2,1)}, u32[]{:S(2)}) copy-start(bf16[2048,924]{0,1:T(8,128)(2,1)} %param.7) | copy-start | bytes 11354116
  229.3 2.4 copy-start.2
  236.3 5.8 %copy-start.6 = (bf16[512,2048]{1,0:T(8,128)(2,1)S(1)}, bf16[512,2048]{1,0:T(8,128)(2,1)}, u32[]{:S(2)}) copy-start(bf16[512,2048]{1,0:T(8,128)(2,1)} %all-gather.5.cloned.1.call-done) | copy-start | bytes 6291460
  242.1 4.1 %copy-start.3 = (f32[512,924]{0,1:T(8,128)S(1)}, f32[512,924]{0,1:T(8,128)}, u32[]{:S(2)}) copy-start(f32[512,924]{0,1:T(8,128)} %get-tuple-element.4) | copy-start | bytes 5677060
  242.1 4.1 %copy-start.4 = (f32[512,924]{0,1:T(8,128)S(1)}, f32[512,924]{0,1:T(8,128)}, u32[]{:S(2)}) copy-start(f32[512,924]{0,1:T(8,128)} %get-tuple-element.6) | copy-start | bytes 5677060
  242.1 4.1 %copy-start.7 = (bf16[512,2048]{1,0:T(8,128)(2,1)S(1)}, bf16[512,2048]{1,0:T(8,128)(2,1)}, u32[]{:S(2)}) copy-start(bf16[512,2048]{1,0:T(8,128)(2,1)} %all-gather.3.cloned.1.call-done) | copy-start | bytes 6291460
Sparse Core Ops, SparseCore 0:
  10.3 46.4 all-gather.4
  59.0 43.2 all-gather.2
  108.5 116.8 all-reduce.2
  236.4 81.9 reduce-scatter.1
where the time goes:
time: 327 us
  waiting for transfers between devices  270 us (83%)
  matrix products  36.7 us (11%)
  between operations  13.8 us (4%)
  other arithmetic  5.43 us (2%)
    psum x1, waiting for transfers between devices, local(): gate, upward, hid_grad = lax.psum((gate_part, up_part, grad_part), 'row')  117 us
    reduce_scatter x1, waiting for transfers between devices, local(): lax.psum_scatter(contract(gate_grad, gate_weight, 1, 1) + contract(up_gra...  68.2 us
    all_gather x1, waiting for transfers between devices, local(): lax.all_gather(tokens, 'col', axis=0, tiled=True)  48.1 us
    all_gather x1, waiting for transfers between devices, local(): lax.all_gather(out_grad, 'col', axis=0, tiled=True)  35.8 us
    dot_general x6, matrix products, contract(): lax.dot_general(left, right, (((left_dim,), (right_dim,)), ((), ())), pre...  27 us
  transfers between devices with their start and end apart: 4, of which 4 were waited for; matrix products, arithmetic and copies ran while one was open for 7% of the time, Pallas kernels for 0%

commit v1 on v0

--- a/solution.py
+++ b/solution.py
@@ -23,7 +23,9 @@
 def local(tokens, out_grad, gate_weight, up_weight, down_weight):
     panel_tokens, panel_grads = (
         lax.all_gather(tokens, "col", axis=0, tiled=True),
-        lax.all_gather(out_grad, "col", axis=0, tiled=True),
+        jnp.concatenate(
+            lax.all_to_all(jnp.stack([out_grad] * lax.axis_size("col")), "col", 0, 0), axis=0
+        ),
     )
     factor = 1.0 / math.sqrt(panel_tokens.shape[0])
     gate_part = jnp.dot(panel_tokens, gate_weight, preferred_element_type=jnp.float32)

time: 327 us -> 294 us (0.90)
  waiting for transfers between devices: 270 us -> 200 us
  blocking collectives: 0 us -> 38.1 us
    all_to_all x0 -> x1, blocking collectives: none -> 38.1 us  [local(): lax.all_to_all(jnp.stack([out_grad] * lax.axis_size('col')), 'col', 0, 0)]
    all_gather x1 -> x0, waiting for transfers between devices: 35.8 us -> none  [local(): lax.all_gather(out_grad, 'col', axis=0, tiled=True)]
    all_gather x1, waiting for transfers between devices: 48.1 us -> 14.1 us  [local(): lax.all_gather(tokens, 'col', axis=0, tiled=True)]
  transfers between devices with their start and end apart: 4 -> 3, of which waited for: 4 -> 3; matrix products, arithmetic and copies ran while one was open for 7% -> 6% of each run, Pallas kernels for 0% -> 0%
where the time goes in v1:
time: 294 us
  waiting for transfers between devices  200 us (68%)
  blocking collectives  38.1 us (13%)
  matrix products  34 us (12%)
  between operations  13.8 us (5%)
  other arithmetic  5.43 us (2%)
    psum x1, waiting for transfers between devices, local(): gate, upward, hid_grad = lax.psum((gate_part, up_part, grad_part), 'row')  117 us
    reduce_scatter x1, waiting for transfers between devices, local(): lax.psum_scatter(contract(gate_grad, gate_weight, 1, 1) + contract(up_gra...  68.2 us
    all_to_all x1, blocking collectives, local(): lax.all_to_all(jnp.stack([out_grad] * lax.axis_size('col')), 'col', 0, 0)  38.1 us
    dot_general x6, matrix products, contract(): lax.dot_general(left, right, (((left_dim,), (right_dim,)), ((), ())), pre...  24.3 us
    all_gather x1, waiting for transfers between devices, local(): lax.all_gather(tokens, 'col', axis=0, tiled=True)  14.1 us
    dot_general x1, matrix products, local(): jnp.dot(panel_tokens, up_weight, preferred_element_type=jnp.float32)  6.27 us
  transfers between devices with their start and end apart: 3, of which 3 were waited for; matrix products, arithmetic and copies ran while one was open for 6% of the time, Pallas kernels for 0%

profile of v1, /device:TPU:0, one launch (start us, length us, event | category | flops | bytes accessed | tf_op | source)
XLA Modules:
  0.0 293.8 jit_solution(18366072808431886036)
XLA Ops:
  7.2 0.0 all-gather.2.cloned.1.call-start
  7.2 0.7 all-gather.2.cloned.1.call-update
  7.9 0.0 all-reduce.3.cloned.1.call-start
  7.9 1.1 stack.2
  9.0 0.0 copy-start.7
  9.0 38.1 %all_to_all.5 = bf16[32,16,2048]{2,1,0:T(8,128)(2,1)S(1)} all-to-all(bf16[32,16,2048]{2,1,0:T(8,128)(2,1)S(1)} %stack.2), channel_id=1, replica_groups=mesh['row'=4,'col'=32] {'col'}, dimensions={0} | all-to-all | bytes 4194304 | tf_op jit(solution)/shard_map/all_to_all | solution.py:27
  47.1 0.0 copy-start.3
  47.2 1.3 copy-done.3
  48.5 0.0 copy-done.7
  48.5 3.4 %fusion.5 = f32[512,924]{0,1:T(8,128)} fusion(bf16[512,2048]{1,0:T(8,128)(2,1)S(1)} %bitcast.20, bf16[924,2048]{1,0:T(8,128)(2,1)S(1)} %copy-done.7), kind=kOutput, calls=%fused_computation.12 | convolution fusion | flops 1937768448 | bytes 7774208 | tf_op jit(solution)/shard_map/dot_general | solution.py:9
  51.9 14.1 %all-gather.2.cloned.1.call-done = bf16[512,2048]{1,0:T(8,128)(2,1)} async-done(((bf16[16,2048]{1,0:T(8,128)(2,1)}), bf16[512,2048]{1,0:T(8,128)(2,1)}) %all-gather.2.cloned.1.call-update) | async-done | bytes 2097168 | tf_op jit(solution)/shard_map/all_gather | solution.py:25
  66.0 0.0 copy-start
  66.0 0.0 copy-start.8
  66.0 6.3 %fusion.6 = f32[512,924]{0,1:T(8,128)} fusion(bf16[512,2048]{1,0:T(8,128)(2,1)} %all-gather.2.cloned.1.call-done, bf16[2048,924]{0,1:T(8,128)(2,1)} %param.8), kind=kOutput, calls=%fused_computation.13 | convolution fusion | flops 1937768448 | bytes 7774208 | tf_op jit(solution)/shard_map/dot_general | solution.py:32
  72.2 0.0 copy-done
  72.2 0.0 copy-done.8
  72.2 3.4 %fusion.7 = f32[512,924]{0,1:T(8,128)} fusion(bf16[512,2048]{1,0:T(8,128)(2,1)S(1)} %copy-done.8, bf16[2048,924]{0,1:T(8,128)(2,1)S(1)} %copy-done), kind=kOutput, calls=%fused_computation.14 | convolution fusion | flops 1937768448 | bytes 7774208 | tf_op jit(solution)/shard_map/dot_general | solution.py:31
  75.6 0.0 all-reduce.3.cloned.1.call-update
  75.7 0.2 reduce-scatter.2.cloned.1.call-start
  75.9 116.8 %all-reduce.3.cloned.1.call-done = (f32[512,924]{0,1:T(8,128)}, f32[512,924]{0,1:T(8,128)}, f32[512,924]{0,1:T(8,128)}) async-done(((f32[512,924]{0,1:T(8,128)}, f32[512,924]{0,1:T(8,128)}, f32[512,924]{0,1:T(8,128)}), (f32[512,924]{0,1:T(8,128)}, f32[512,924]{0,1:T(8,128)}, f32[512,924]{0,1:T(8,128)})) %all-reduce.3.cloned.1.call-update) | async-done | bytes 5677072 | tf_op jit(solution)/shard_map/psum | solution.py:34
  192.7 0.0 copy-start.1
  192.7 3.9 %multiply_convert_fusion.4 = (bf16[512,924]{0,1:T(8,128)(2,1)S(1)}, bf16[512,924]{0,1:T(8,128)(2,1)S(1)}) fusion(f32[512,924]{0,1:T(8,128)} %get-tuple-element.5, f32[512,924]{0,1:T(8,128)} %get-tuple-element.4, f32[512,924]{0,1:T(8,128)} %get-tuple-element.6), kind=kLoop, calls=%fused_computation.7 | loop fusion | flops 6150144 | bytes 7569408 | tf_op jit(solution)/shard_map/convert_element_type | solution.py:19
  196.6 0.0 copy-done.1
  196.6 0.0 copy-start.2
  196.6 2.4 fusion.8
  199.0 0.0 copy-done.2
  199.0 4.5 %convolution_add_fusion = f32[512,2048]{1,0:T(8,128)} fusion(f32[512,2048]{1,0:T(8,128)S(1)} %fusion.8, bf16[512,924]{0,1:T(8,128)(2,1)S(1)} %get-tuple-element.7, bf16[2048,924]{0,1:T(8,128)(2,1)S(1)} %copy-done.2), kind=kOutput, calls=%fused_computation.5 | convolution fusion | flops 1938817024 | bytes 13119488 | tf_op jit(solution)/shard_map/dot_general | solution.py:9
  203.6 0.0 reduce-scatter.2.cloned.1.call-update
  203.6 0.0 copy-start.9
  203.6 5.8 %fusion = bf16[2048,924]{0,1:T(8,128)(2,1)} fusion(bf16[512,924]{0,1:T(8,128)(2,1)S(1)} %get-tuple-element.8, bf16[512,2048]{1,0:T(8,128)(2,1)} %all-gather.2.cloned.1.call-done), kind=kOutput, calls=%fused_computation.3 | convolution fusion | flops 1941553152 | bytes 6828032 | tf_op jit(solution)/shard_map/dot_general | solution.py:9
  209.3 0.0 copy-done.9
  209.4 0.0 copy-start.4
  209.4 0.0 copy-start.5
  209.4 0.0 copy-start.6
  209.4 4.1 %fusion.1 = bf16[2048,924]{0,1:T(8,128)(2,1)} fusion(bf16[512,924]{0,1:T(8,128)(2,1)S(1)} %get-tuple-element.7, bf16[512,2048]{1,0:T(8,128)(2,1)S(1)} %copy-done.9), kind=kOutput, calls=%fused_computation.4 | convolution fusion | flops 1941553152 | bytes 6828032 | tf_op jit(solution)/shard_map/dot_general | solution.py:9
  213.4 0.0 copy-done.4
  213.4 0.0 copy-done.5
  213.4 0.0 copy-done.6
  213.4 4.1 %multiply_convert_fusion = bf16[924,2048]{1,0:T(8,128)(2,1)} fusion(bf16[512,2048]{1,0:T(8,128)(2,1)S(1)} %bitcast.21, f32[512,924]{0,1:T(8,128)S(1)} %copy-done.6, f32[512,924]{0,1:T(8,128)S(1)} %copy-done.5), kind=kOutput, calls=%fused_computation | convolution fusion | flops 1944391680 | bytes 9666560 | tf_op jit(solution)/shard_map/dot_general | solution.py:9
  217.5 68.2 %reduce-scatter.2.cloned.1.call-done = f32[16,2048]{1,0:T(8,128)} async-done(((f32[512,2048]{1,0:T(8,128)}), f32[16,2048]{1,0:T(8,128)}) %reduce-scatter.2.cloned.1.call-update) | async-done | bytes 131088 | tf_op jit(solution)/shard_map/reduce_scatter | solution.py:36
  285.8 1.5 convert_element_type.29
Async XLA Ops:
  7.2 58.8 %all-gather.2.cloned.1.call-start = ((), (), s32[]{:S(2)}) async-start(), calls=%async_computation.2 | async-start | bytes 2162688 | tf_op jit(solution)/shard_map/all_gather | solution.py:25
  7.9 184.8 %all-reduce.3.cloned.1.call-start = ((), (), s32[]{:S(2)}) async-start(), calls=%async_computation.4 | async-start | bytes 11403264 | tf_op jit(solution)/shard_map/psum | solution.py:34
  9.0 39.4 %copy-start.7 = (bf16[924,2048]{1,0:T(8,128)(2,1)S(1)}, bf16[924,2048]{1,0:T(8,128)(2,1)}, u32[]{:S(2)}) copy-start(bf16[924,2048]{1,0:T(8,128)(2,1)} %param.9) | copy-start | bytes 11354116
  47.1 1.3 copy-start.3
  66.0 6.3 %copy-start = (bf16[2048,924]{0,1:T(8,128)(2,1)S(1)}, bf16[2048,924]{0,1:T(8,128)(2,1)}, u32[]{:S(2)}) copy-start(bf16[2048,924]{0,1:T(8,128)(2,1)} %param.7) | copy-start | bytes 11354116
  66.0 6.3 %copy-start.8 = (bf16[512,2048]{1,0:T(8,128)(2,1)S(1)}, bf16[512,2048]{1,0:T(8,128)(2,1)}, u32[]{:S(2)}) copy-start(bf16[512,2048]{1,0:T(8,128)(2,1)} %all-gather.2.cloned.1.call-done) | copy-start | bytes 6291460
  75.7 210.1 %reduce-scatter.2.cloned.1.call-start = ((), (), s32[]{:S(2)}) async-start(), calls=%async_computation.3 | async-start | bytes 4325376 | tf_op jit(solution)/shard_map/reduce_scatter | solution.py:36
  192.7 3.9 %copy-start.1 = (bf16[2048,924]{0,1:T(8,128)(2,1)S(1)}, bf16[2048,924]{0,1:T(8,128)(2,1)}, u32[]{:S(2)}) copy-start(bf16[2048,924]{0,1:T(8,128)(2,1)} %param.7) | copy-start | bytes 11354116
  196.6 2.4 copy-start.2
  203.6 5.8 %copy-start.9 = (bf16[512,2048]{1,0:T(8,128)(2,1)S(1)}, bf16[512,2048]{1,0:T(8,128)(2,1)}, u32[]{:S(2)}) copy-start(bf16[512,2048]{1,0:T(8,128)(2,1)} %all-gather.2.cloned.1.call-done) | copy-start | bytes 6291460
  209.4 4.1 %copy-start.4 = (bf16[32,16,2048]{2,1,0:T(8,128)(2,1)S(1)}, bf16[32,16,2048]{2,1,0:T(8,128)(2,1)}, u32[]{:S(2)}) copy-start(bf16[32,16,2048]{2,1,0:T(8,128)(2,1)} %copy-done.3) | copy-start | bytes 6291460
  209.4 4.1 %copy-start.5 = (f32[512,924]{0,1:T(8,128)S(1)}, f32[512,924]{0,1:T(8,128)}, u32[]{:S(2)}) copy-start(f32[512,924]{0,1:T(8,128)} %get-tuple-element.4) | copy-start | bytes 5677060
  209.4 4.1 %copy-start.6 = (f32[512,924]{0,1:T(8,128)S(1)}, f32[512,924]{0,1:T(8,128)}, u32[]{:S(2)}) copy-start(f32[512,924]{0,1:T(8,128)} %get-tuple-element.6) | copy-start | bytes 5677060
Sparse Core Ops, SparseCore 0:
  10.3 55.6 all-gather.1
  75.8 116.8 all-reduce.2
  203.7 82.0 reduce-scatter.1
